TPU v7x, 512 devices: a whole 4x4x16 slice. The times are simulated.
512 devices in a mesh: tm: 16 (over z), query: 8 (over y, core), rec: 4 (over x).
Axes of the slice: x: 4, y: 4, z: 16, core: 2. Of those that a mesh axis runs over, the one named last changes fastest.
Arguments:
- frames: bfloat16 [4, 8192, 1024], P('rec', 'tm'), may hold values from -100 to 100
- queries: bfloat16 [4096, 1024], P('query'), may hold values from -10 to 10
- kernel: float32 [33, 4096], P(None, 'query'), may hold values from 0.01 to 0.12
- labels: int32 [4, 8192], P('rec', 'tm'), may hold values from 0 to 4095
- lengths: int32 [4], P('rec'), may hold values from 2048 to 8192, as said below
Outputs:
- grad_frames: bfloat16 [4, 8192, 1024], P('rec', 'tm', 'query')
- grad_queries: bfloat16 [4096, 1024], P('query', 'rec')
- grad_kernel: float32 [33, 4096], P(None, 'query')
Inputs may be any that keep to these rules, and one draw needn't show every extreme that they name: `lengths`: each entry counts the valid frames at the start of its recording; at least one recording has all 8192 frames valid.
All inputs are finite; a program needn't handle non-finite values.
Results may differ from a plain program's by a relative error of at most 0.0049.
Values sent between devices are 32-bit elements; how exact they have to be, the bound alone decides.
No kernel may reach another device: no remote copies, remote signals or barrier semaphores. Data moves between devices by JAX's collectives and lax.ppermute only.
A program may use at most 64 MiB of HBM per device.

v0:
```python
import math
import jax
import jax.numpy as jnp
from jax import lax
from jax.sharding import PartitionSpec as P


def merged(x, axis, combine):
    everything = jax.tree.map(lambda part: lax.all_gather(part, axis), x)
    first = jax.tree.map(lambda part: part[0], everything)

    def step(k, so_far):
        return combine(so_far, jax.tree.map(lambda part: part[k], everything))

    return lax.fori_loop(1, lax.axis_size(axis), step, first)


def with_halo(x, sides, width):
    for axis, dim in sides:
        peers, length = (lax.axis_size(axis), x.shape[dim])
        up = [(i, (i + 1) % peers) for i in range(peers - 1)]
        down = [(j, i) for i, j in up]
        last = lax.slice_in_dim(x, length - width, length, axis=dim)
        first = lax.slice_in_dim(x, 0, width, axis=dim)
        before = lax.ppermute(last, axis, up)
        after = lax.ppermute(first, axis, down)
        x = jnp.concatenate([before, x, after], axis=dim)
    return x


def tap_sum(kernel, padded, row_count, flipped):
    tap_count = kernel.shape[0]
    running = jnp.zeros((row_count, padded.shape[1]), jnp.float32)
    for offset in range(tap_count):
        begin_row = tap_count - 1 - offset if flipped else offset
        running = running + kernel[offset][None, :] * padded[begin_row : begin_row + row_count]
    return running


def combine_stats(first_pair, second_pair):
    top_value = jnp.maximum(first_pair[0], second_pair[0])
    total_value = first_pair[1] * jnp.exp(first_pair[0] - top_value) + second_pair[1] * jnp.exp(
        second_pair[0] - top_value
    )
    return (top_value, total_value)


def row_softmax(smooth):
    local_top = jnp.max(smooth, axis=1)
    local_total = jnp.sum(jnp.exp(smooth - local_top[:, None]), axis=1)
    top_value, total_value = merged((local_top, local_total), "query", combine_stats)
    return jnp.exp(smooth - top_value[:, None]) / total_value[:, None]


def per_device(frames, queries, kernel, labels, lengths):
    frame_rows = frames[0]
    label_ids = labels[0]
    length_now = lengths[0]
    row_count = frame_rows.shape[0]
    query_count = queries.shape[0]
    width = frame_rows.shape[1]
    tap_count = kernel.shape[0]
    rim_width = tap_count // 2
    logit_scale = 10.0 / math.sqrt(width)
    frame_start = lax.axis_index("tm") * row_count
    is_valid = frame_start + jnp.arange(row_count, dtype=jnp.int32) < length_now
    query_start = lax.axis_index("query") * query_count
    query_ids = query_start + jnp.arange(query_count, dtype=jnp.int32)
    scores = (
        lax.dot_general(
            frame_rows, queries, (((1,), (1,)), ((), ())), preferred_element_type=jnp.float32
        )
        * logit_scale
    )
    scores = jnp.where(is_valid[:, None], scores, 0.0)
    padded = with_halo(scores, (("tm", 0),), rim_width)
    smooth = tap_sum(kernel, padded, row_count, False)
    softmax_out = row_softmax(smooth)
    positive = (label_ids[:, None] == query_ids[None, :]).astype(jnp.float32)
    map_grad = jnp.where(is_valid[:, None], softmax_out - positive, 0.0)
    grad_pad = with_halo(map_grad, (("tm", 0),), rim_width)
    score_grad = tap_sum(kernel, grad_pad, row_count, True)
    score_grad = jnp.where(is_valid[:, None], score_grad, 0.0).astype(jnp.bfloat16)
    frame_part = jnp.dot(score_grad, queries, preferred_element_type=jnp.float32)
    frame_sum = lax.psum_scatter(frame_part, "query", scatter_dimension=1, tiled=True)
    grad_frames = (frame_sum * logit_scale).astype(jnp.bfloat16)[None]
    query_part = lax.dot_general(
        score_grad, frame_rows, (((0,), (0,)), ((), ())), preferred_element_type=jnp.float32
    )
    kernel_part = jnp.stack(
        [
            jnp.sum(map_grad * padded[offset : offset + row_count], axis=0)
            for offset in range(tap_count)
        ]
    )
    query_whole, grad_kernel = lax.psum((query_part, kernel_part), ("tm", "rec"))
    col_count = width // lax.axis_size("rec")
    query_cols = lax.dynamic_slice_in_dim(
        query_whole, lax.axis_index("rec") * col_count, col_count, 1
    )
    grad_queries = (query_cols * logit_scale).astype(jnp.bfloat16)
    return (grad_frames, grad_queries, grad_kernel)


def solution(mesh):
    in_specs = (P("rec", "tm", None), P("query", None), P(None, "query"), P("rec", "tm"), P("rec"))
    out_specs = (P("rec", "tm", "query"), P("query", "rec"), P(None, "query"))
    return jax.shard_map(
        per_device, mesh=mesh, in_specs=in_specs, out_specs=out_specs, check_vma=False
    )
```

profile of v0, /device:TPU:8, one launch (start us, length us, event | category | flops | bytes accessed | tf_op | source)
XLA Modules:
  0.0 376.1 jit_solution(3690222084819182365)
XLA Ops:
  8.0 0.0 copy-start
  8.0 0.0 all-reduce.3.cloned.1.call-start
  8.8 0.4 copy-done
  9.2 2.0 fusion
  11.3 3.8 %collective-permute-start = (f32[16,512]{1,0:T(8,128)S(1)}, f32[16,512]{1,0:T(8,128)S(1)}, u32[]{:S(2)}, u32[]{:S(2)}) collective-permute-start(f32[16,512]{1,0:T(8,128)S(1)} %get-tuple-element.192), channel_id=1, source_target_pairs={{0,32},{32,64},{64,96},{96,128},{128,160},{160,192},{192,224},{224... | collective-permute-start | bytes 98312 | tf_op jit(solution)/shard_map/ppermute | solution.py:25
  15.1 1.3 collective-permute-start.1
  16.5 0.2 collective-permute-done
  16.7 4.2 %collective-permute-done.1 = f32[16,512]{1,0:T(8,128)S(1)} collective-permute-done((f32[16,512]{1,0:T(8,128)S(1)}, f32[16,512]{1,0:T(8,128)S(1)}, u32[]{:S(2)}, u32[]{:S(2)}) %collective-permute-start.1) | collective-permute-done | bytes 32800 | tf_op jit(solution)/shard_map/ppermute | solution.py:26
  20.9 5.1 %fusion.131 = (f32[512]{0:T(512)S(1)}, f32[512,512]{1,0:T(8,128)S(1)}) fusion(f32[16,512]{1,0:T(8,128)S(1)} %collective-permute-done.1, f32[512,512]{1,0:T(8,128)S(1)} %fusion, f32[512]{0:T(512)S(1)} %bitcast.126, f32[512]{0:T(512)S(1)} %bitcast.128, f32[512]{0:T(512)S(1)} %bitcast.132, f32[512]{0:T(512)S(1)} %bitcast.134, f32[512]{0:T(512)S(1)} %bitcast.136, ...), kind=kLoop, calls=%fused_computation.265 | loop fusion | flops 25689600 | bytes 2232320 | tf_op jit(solution)/shard_map/reduce_max | solution.py:49
  26.1 1.0 copy-done.1
  27.0 0.3 exponential_reduce_fusion
  27.3 12.2 %all-gather.3 = f32[8,1,512]{2,1,0:T(1,128)S(1)} all-gather(f32[1,1,512]{2,1,0:T(1,128)S(1)} %bitcast.194), channel_id=3, replica_groups=mesh['tm'=16,'query'=8,'rec'=4] {'query'}, dimensions={0}, use_global_device_ids=true | all-gather | bytes 18432 | tf_op jit(solution)/shard_map/all_gather | solution.py:9
  39.5 12.0 %all-gather.2 = f32[8,1,512]{2,1,0:T(1,128)S(1)} all-gather(f32[1,1,512]{2,1,0:T(1,128)S(1)} %bitcast.168), channel_id=2, replica_groups=mesh['tm'=16,'query'=8,'rec'=4] {'query'}, dimensions={0}, use_global_device_ids=true | all-gather | bytes 18432 | tf_op jit(solution)/shard_map/all_gather | solution.py:9
  51.4 0.4 while.17
  51.8 4.3 %multiply_reduce_fusion = (f32[512]{0:T(512)S(1)}, f32[512]{0:T(512)S(1)}, f32[512]{0:T(512)S(1)}, f32[512]{0:T(512)S(1)}, f32[512]{0:T(512)S(1)}, /*index=5*/f3...) fusion(f32[16,512]{1,0:T(8,128)S(1)} %collective-permute-done.1, ...), kind=kLoop, calls=%fused_computation.222 | loop fusion | flops 8646144 | bytes 3205632 | tf_op jit(solution)/shard_map/reduce_sum | solution.py:92
  56.1 1.3 collective-permute-start.2
  57.4 4.5 %collective-permute-start.3 = (f32[16,512]{1,0:T(8,128)S(1)}, f32[16,512]{1,0:T(8,128)S(1)}, u32[]{:S(2)}, u32[]{:S(2)}) collective-permute-start(f32[16,512]{1,0:T(8,128)S(1)} %get-tuple-element.191), channel_id=1, source_target_pairs={{0,32},{32,64},{64,96},{96,128},{128,160},{160,192},{192,224},{224... | collective-permute-start | bytes 98312 | tf_op jit(solution)/shard_map/ppermute | solution.py:25
  62.0 1.9 multiply_reduce_fusion.1
  63.9 1.2 multiply_reduce_fusion.17
  65.1 1.0 multiply_reduce_fusion.26
  66.1 3.9 %stack.135 = f32[33,512]{1,0:T(8,128)} concatenate(f32[1,512]{1,0:T(1,128)S(1)} %bitcast.193, f32[1,512]{1,0:T(1,128)S(1)} %bitcast.192, f32[1,512]{1,0:T(1,128)S(1)} %bitcast.191, f32[1,512]{1,0:T(1,128)S(1)} %bitcast.190, f32[1,512]{1,0:T(1,128)S(1)} %bitcast.189, f32[1,512]{1,0:T(1,128)S(1)} %bitcast.188, f32[1,512]{1,0:T(1,128)S(1)} %bitcast.187, f32[1,512]{1,0:T(1,128)S(1)} %bitcast.186, ...), dimensions={0} | concatenate | bytes 135168 | tf_op jit(solution)/shard_map/stack | solution.py:90
  70.0 8.6 %fusion.6 = bf16[512,512]{1,0:T(8,128)(2,1)S(1)} fusion(f32[16,512]{1,0:T(8,128)S(1)} %collective-permute-done.3, f32[16,512]{1,0:T(8,128)S(1)} %collective-permute-done.2, f32[512,512]{1,0:T(8,128)S(1)} %get-tuple-element.185, f32[512]{0:T(512)S(1)} %bitcast.127, f32[512]{0:T(512)S(1)} %bitcast.129, f32[512]{0:T(512)S(1)} %bitcast.133, ...), kind=kLoop, calls=%fused_computation.70 | loop fusion | flops 25952256 | bytes 1706496 | tf_op jit(solution)/shard_map/convert_element_type | solution.py:83
  78.5 2.0 fusion.127
  80.6 0.0 all-reduce.3.cloned.1.call-update
  80.6 0.0 reduce-scatter.2.cloned.1.call-start
  80.7 1.1 copy-done.2
  81.8 2.0 fusion.136
  83.9 0.0 reduce-scatter.2.cloned.1.call-update
  83.9 280.7 %all-reduce.3.cloned.1.call-done = (f32[512,1024]{1,0:T(8,128)}, f32[33,512]{1,0:T(8,128)}) async-done(((f32[512,1024]{1,0:T(8,128)}, f32[33,512]{1,0:T(8,128)}), (f32[512,1024]{1,0:T(8,128)}, f32[33,512]{1,0:T(8,128)})) %all-reduce.3.cloned.1.call-update) | async-done | bytes 2164752 | tf_op jit(solution)/shard_map/psum | solution.py:96
  364.6 1.8 multiply_convert_fusion
  366.4 1.6 fusion.130
  368.1 0.6 copy.26
  (37 shorter events, 0.3 us)
Async XLA Ops:
  8.0 1.2 copy-start
  8.0 356.6 %all-reduce.3.cloned.1.call-start = ((), (), s32[]{:S(2)}) async-start(), calls=%async_computation.2 | async-start | bytes 4358144 | tf_op jit(solution)/shard_map/psum | solution.py:96
  9.2 42.6 %copy-start.5 = (pred[512]{0:T(512)(128)(4,1)}, pred[512]{0:T(512)(128)(4,1)S(1)}, u32[]{:S(2)}) copy-start(pred[512]{0:T(512)(128)(4,1)S(1)} %add_compare_fusion) | copy-start | bytes 1540
  9.2 7.2 %copy-start.4 = (f32[33,512]{1,0:T(8,128)S(1)}, f32[33,512]{1,0:T(8,128)}, u32[]{:S(2)}) copy-start(f32[33,512]{1,0:T(8,128)} %param.9) | copy-start | bytes 202756
  11.3 5.4 %collective-permute-start = (f32[16,512]{1,0:T(8,128)S(1)}, f32[16,512]{1,0:T(8,128)S(1)}, u32[]{:S(2)}, u32[]{:S(2)}) collective-permute-start(f32[16,512]{1,0:T(8,128)S(1)} %get-tuple-element.192), channel_id=1, source_target_pairs={{0,32},{32,64},{64,96},{96,128},{128,160},{160,192},{192,224},{224... | collective-permute-start | bytes 98312 | tf_op jit(solution)/shard_map/ppermute | solution.py:25
  15.1 5.8 %collective-permute-start.1 = (f32[16,512]{1,0:T(8,128)S(1)}, f32[16,512]{1,0:T(8,128)S(1)}, u32[]{:S(2)}, u32[]{:S(2)}) collective-permute-start(f32[16,512]{1,0:T(8,128)S(1)} %get-tuple-element.193), channel_id=1, source_target_pairs={{32,0},{64,32},{96,64},{128,96},{160,128},{192,160},{224,192},{256... | collective-permute-start | bytes 98312 | tf_op jit(solution)/shard_map/ppermute | solution.py:26
  26.0 1.0 copy-start.1
  26.0 25.8 %copy-start.6 = (s32[1,512]{1,0:T(1,128)S(1)}, s32[1,512]{1,0:T(1,128)}, u32[]{:S(2)}) copy-start(s32[1,512]{1,0:T(1,128)} %param.10) | copy-start | bytes 6148
  56.1 13.9 %collective-permute-start.2 = (f32[16,512]{1,0:T(8,128)S(1)}, f32[16,512]{1,0:T(8,128)S(1)}, u32[]{:S(2)}, u32[]{:S(2)}) collective-permute-start(f32[16,512]{1,0:T(8,128)S(1)} %get-tuple-element.190), channel_id=1, source_target_pairs={{32,0},{64,32},{96,64},{128,96},{160,128},{192,160},{224,192},{256... | collective-permute-start | bytes 98312 | tf_op jit(solution)/shard_map/ppermute | solution.py:26
  57.4 12.6 %collective-permute-start.3 = (f32[16,512]{1,0:T(8,128)S(1)}, f32[16,512]{1,0:T(8,128)S(1)}, u32[]{:S(2)}, u32[]{:S(2)}) collective-permute-start(f32[16,512]{1,0:T(8,128)S(1)} %get-tuple-element.191), channel_id=1, source_target_pairs={{0,32},{32,64},{64,96},{96,128},{128,160},{160,192},{192,224},{224... | collective-permute-start | bytes 98312 | tf_op jit(solution)/shard_map/ppermute | solution.py:25
  80.6 1.2 copy-start.2
  80.6 285.8 %reduce-scatter.2.cloned.1.call-start = ((), (), s32[]{:S(2)}) async-start(), calls=%async_computation.1 | async-start | bytes 2359296 | tf_op jit(solution)/shard_map/reduce_scatter | solution.py:85
  364.6 3.4 copy-start.3
Sparse Core Ops, SparseCore 0:
  80.7 283.8 all-reduce.2
Sparse Core Ops, SparseCore 1:
  84.0 42.4 reduce-scatter.1
where the time goes:
time: 377 us; the launch traced here: 376 us
  waiting for transfers between devices  285 us (76%)
  other arithmetic  25.9 us (7%)
  blocking collectives  24.1 us (6%)
  between operations  16.4 us (4%)
  starting transfers between devices  11 us (3%)
  local copies, waits for them, and re-layouts  7.24 us (2%)
  matrix products  6.07 us (2%)
    psum x1, waiting for transfers between devices, per_device(): lax.psum((query_part, kernel_part), ('tm', 'rec'))  281 us
    all_gather x2, blocking collectives, merged(): everything = jax.tree.map(lambda part: lax.all_gather(part, axis), x)  24.1 us
    convert_element_type x1, other arithmetic, per_device(): jnp.where(is_valid[:, None], score_grad, 0.0).astype(jnp.bfloat16)  8.56 us
    ppermute x2, starting transfers between devices, with_halo(): before = lax.ppermute(last, axis, up)  8.38 us
    reduce_sum x4, other arithmetic, per_device(): jnp.sum(map_grad * padded[offset:offset + row_count], axis=0)  8.36 us
  transfers between devices with their start and end apart: 6, of which 3 were waited for; matrix products, arithmetic and copies ran while one was open for 3% of the time, Pallas kernels for 0%

commit v1 on v0

--- a/solution.py
+++ b/solution.py
@@ -3,6 +3,11 @@
 import jax.numpy as jnp
 from jax import lax
 from jax.sharding import PartitionSpec as P
+
+
+def one_after_other(array, one, other):
+    inner = lax.psum(array, one)
+    return lax.psum(inner, other)
 
 
 def merged(x, axis, combine):
@@ -93,7 +98,7 @@
             for offset in range(tap_count)
         ]
     )
-    query_whole, grad_kernel = lax.psum((query_part, kernel_part), ("tm", "rec"))
+    query_whole, grad_kernel = one_after_other((query_part, kernel_part), "tm", "rec")
     col_count = width // lax.axis_size("rec")
     query_cols = lax.dynamic_slice_in_dim(
         query_whole, lax.axis_index("rec") * col_count, col_count, 1

time: 377 us -> 316 us (0.84)
  the two profiles are of different devices: /device:TPU:8 before, /device:TPU:1 now
where the time goes in v1:
time: 316 us
  waiting for transfers between devices  221 us (70%)
  blocking collectives  27.1 us (9%)
  other arithmetic  25.9 us (8%)
  between operations  16.4 us (5%)
  starting transfers between devices  11.1 us (4%)
  local copies, waits for them, and re-layouts  8.12 us (3%)
  matrix products  6.08 us (2%)
    psum x1, waiting for transfers between devices, one_after_other(): inner = lax.psum(array, one)  136 us
    psum x1, waiting for transfers between devices, one_after_other(): return lax.psum(inner, other)  81.3 us
    all_gather x2, blocking collectives, merged(): everything = jax.tree.map(lambda part: lax.all_gather(part, axis), x)  27.1 us
    convert_element_type x1, other arithmetic, per_device(): jnp.where(is_valid[:, None], score_grad, 0.0).astype(jnp.bfloat16)  8.56 us
    reduce_sum x4, other arithmetic, per_device(): jnp.sum(map_grad * padded[offset:offset + row_count], axis=0)  8.36 us
    ppermute x2, starting transfers between devices, with_halo(): before = lax.ppermute(last, axis, up)  8.36 us
  transfers between devices with their start and end apart: 7, of which 3 were waited for; matrix products, arithmetic and copies ran while one was open for 4% of the time, Pallas kernels for 0%

profile of v1, /device:TPU:1, one launch (start us, length us, event | category | flops | bytes accessed | tf_op | source)
XLA Modules:
  0.0 315.8 jit_solution(17812967029710396932)
XLA Ops:
  8.0 0.0 all-reduce.5.cloned.1.call-start
  8.8 0.4 copy-done
  9.2 2.0 fusion
  11.3 4.4 %collective-permute-start = (f32[16,512]{1,0:T(8,128)S(1)}, f32[16,512]{1,0:T(8,128)S(1)}, u32[]{:S(2)}, u32[]{:S(2)}) collective-permute-start(f32[16,512]{1,0:T(8,128)S(1)} %get-tuple-element.194), channel_id=1, source_target_pairs={{0,32},{32,64},{64,96},{96,128},{128,160},{160,192},{192,224},{224... | collective-permute-start | bytes 98312 | tf_op jit(solution)/shard_map/ppermute | solution.py:30
  15.7 1.3 collective-permute-start.1
  17.1 3.4 %collective-permute-done.1 = f32[16,512]{1,0:T(8,128)S(1)} collective-permute-done((f32[16,512]{1,0:T(8,128)S(1)}, f32[16,512]{1,0:T(8,128)S(1)}, u32[]{:S(2)}, u32[]{:S(2)}) %collective-permute-start.1) | collective-permute-done | bytes 32800 | tf_op jit(solution)/shard_map/ppermute | solution.py:31
  20.5 5.1 %fusion.131 = (f32[512]{0:T(512)S(1)}, f32[512,512]{1,0:T(8,128)S(1)}) fusion(f32[16,512]{1,0:T(8,128)S(1)} %collective-permute-done.1, f32[512,512]{1,0:T(8,128)S(1)} %fusion, f32[512]{0:T(512)S(1)} %bitcast.126, f32[512]{0:T(512)S(1)} %bitcast.128, f32[512]{0:T(512)S(1)} %bitcast.132, f32[512]{0:T(512)S(1)} %bitcast.134, f32[512]{0:T(512)S(1)} %bitcast.136, ...), kind=kLoop, calls=%fused_computation.265 | loop fusion | flops 25689600 | bytes 2232320 | tf_op jit(solution)/shard_map/reduce_max | solution.py:54
  25.6 1.0 copy-done.1
  26.6 0.3 exponential_reduce_fusion
  26.9 15.8 %all-gather.3 = f32[8,1,512]{2,1,0:T(1,128)S(1)} all-gather(f32[1,1,512]{2,1,0:T(1,128)S(1)} %bitcast.194), channel_id=3, replica_groups=mesh['tm'=16,'query'=8,'rec'=4] {'query'}, dimensions={0}, use_global_device_ids=true | all-gather | bytes 18432 | tf_op jit(solution)/shard_map/all_gather | solution.py:14
  42.7 11.3 %all-gather.2 = f32[8,1,512]{2,1,0:T(1,128)S(1)} all-gather(f32[1,1,512]{2,1,0:T(1,128)S(1)} %bitcast.168), channel_id=2, replica_groups=mesh['tm'=16,'query'=8,'rec'=4] {'query'}, dimensions={0}, use_global_device_ids=true | all-gather | bytes 18432 | tf_op jit(solution)/shard_map/all_gather | solution.py:14
  54.0 0.4 while.17
  54.4 4.3 %multiply_reduce_fusion = (f32[512]{0:T(512)S(1)}, f32[512]{0:T(512)S(1)}, f32[512]{0:T(512)S(1)}, f32[512]{0:T(512)S(1)}, f32[512]{0:T(512)S(1)}, /*index=5*/f3...) fusion(f32[16,512]{1,0:T(8,128)S(1)} %collective-permute-done.1, ...), kind=kLoop, calls=%fused_computation.222 | loop fusion | flops 8646144 | bytes 3205632 | tf_op jit(solution)/shard_map/reduce_sum | solution.py:97
  58.7 1.3 collective-permute-start.2
  60.0 4.0 %collective-permute-start.3 = (f32[16,512]{1,0:T(8,128)S(1)}, f32[16,512]{1,0:T(8,128)S(1)}, u32[]{:S(2)}, u32[]{:S(2)}) collective-permute-start(f32[16,512]{1,0:T(8,128)S(1)} %get-tuple-element.193), channel_id=1, source_target_pairs={{0,32},{32,64},{64,96},{96,128},{128,160},{160,192},{192,224},{224... | collective-permute-start | bytes 98312 | tf_op jit(solution)/shard_map/ppermute | solution.py:30
  64.0 1.9 multiply_reduce_fusion.1
  65.9 1.2 multiply_reduce_fusion.17
  67.1 1.0 multiply_reduce_fusion.26
  68.1 3.9 %stack.135 = f32[33,512]{1,0:T(8,128)} concatenate(f32[1,512]{1,0:T(1,128)S(1)} %bitcast.193, f32[1,512]{1,0:T(1,128)S(1)} %bitcast.192, f32[1,512]{1,0:T(1,128)S(1)} %bitcast.191, f32[1,512]{1,0:T(1,128)S(1)} %bitcast.190, f32[1,512]{1,0:T(1,128)S(1)} %bitcast.189, f32[1,512]{1,0:T(1,128)S(1)} %bitcast.188, f32[1,512]{1,0:T(1,128)S(1)} %bitcast.187, f32[1,512]{1,0:T(1,128)S(1)} %bitcast.186, ...), dimensions={0} | concatenate | bytes 135168 | tf_op jit(solution)/shard_map/stack | solution.py:95
  72.0 8.6 %fusion.6 = bf16[512,512]{1,0:T(8,128)(2,1)S(1)} fusion(f32[16,512]{1,0:T(8,128)S(1)} %collective-permute-done.3, f32[16,512]{1,0:T(8,128)S(1)} %collective-permute-done.2, f32[512,512]{1,0:T(8,128)S(1)} %get-tuple-element.187, f32[512]{0:T(512)S(1)} %bitcast.127, f32[512]{0:T(512)S(1)} %bitcast.129, f32[512]{0:T(512)S(1)} %bitcast.133, ...), kind=kLoop, calls=%fused_computation.70 | loop fusion | flops 25952256 | bytes 1706496 | tf_op jit(solution)/shard_map/convert_element_type | solution.py:88
  80.6 2.0 fusion.127
  82.6 0.0 reduce-scatter.2.cloned.1.call-start
  82.7 1.1 copy-done.2
  83.8 2.0 fusion.136
  85.9 0.0 reduce-scatter.2.cloned.1.call-update
  85.9 0.0 all-reduce.7.cloned.1.call-start
  85.9 136.1 %all-reduce.5.cloned.1.call-done = (f32[512,1024]{1,0:T(8,128)}, f32[33,512]{1,0:T(8,128)}) async-done(((f32[512,1024]{1,0:T(8,128)}, f32[33,512]{1,0:T(8,128)}), (f32[512,1024]{1,0:T(8,128)}, f32[33,512]{1,0:T(8,128)})) %all-reduce.5.cloned.1.call-update) | async-done | bytes 2164752 | tf_op jit(solution)/shard_map/psum | solution.py:9
  222.0 0.0 reduce-scatter.2.cloned.1.call-done
  222.1 1.6 fusion.130
  223.7 81.3 %all-reduce.7.cloned.1.call-done = (f32[512,1024]{1,0:T(8,128)}, f32[33,512]{1,0:T(8,128)}) async-done(((f32[512,1024]{1,0:T(8,128)}, f32[33,512]{1,0:T(8,128)}), (f32[512,1024]{1,0:T(8,128)}, f32[33,512]{1,0:T(8,128)})) %all-reduce.7.cloned.1.call-update) | async-done | bytes 2164752 | tf_op jit(solution)/shard_map/psum | solution.py:10
  305.0 1.8 multiply_convert_fusion
  306.8 1.5 copy.28
  (38 shorter events, 0.4 us)
Async XLA Ops:
  8.0 1.2 copy-start
  8.0 214.0 %all-reduce.5.cloned.1.call-start = ((), (), s32[]{:S(2)}) async-start(), calls=%async_computation.2 | async-start | bytes 4358144 | tf_op jit(solution)/shard_map/psum | solution.py:9
  9.2 45.2 %copy-start.4 = (pred[512]{0:T(512)(128)(4,1)}, pred[512]{0:T(512)(128)(4,1)S(1)}, u32[]{:S(2)}) copy-start(pred[512]{0:T(512)(128)(4,1)S(1)} %add_compare_fusion) | copy-start | bytes 1540
  9.2 7.7 %copy-start.3 = (f32[33,512]{1,0:T(8,128)S(1)}, f32[33,512]{1,0:T(8,128)}, u32[]{:S(2)}) copy-start(f32[33,512]{1,0:T(8,128)} %param.9) | copy-start | bytes 202756
  11.3 5.8 %collective-permute-start = (f32[16,512]{1,0:T(8,128)S(1)}, f32[16,512]{1,0:T(8,128)S(1)}, u32[]{:S(2)}, u32[]{:S(2)}) collective-permute-start(f32[16,512]{1,0:T(8,128)S(1)} %get-tuple-element.194), channel_id=1, source_target_pairs={{0,32},{32,64},{64,96},{96,128},{128,160},{160,192},{192,224},{224... | collective-permute-start | bytes 98312 | tf_op jit(solution)/shard_map/ppermute | solution.py:30
  15.7 4.8 %collective-permute-start.1 = (f32[16,512]{1,0:T(8,128)S(1)}, f32[16,512]{1,0:T(8,128)S(1)}, u32[]{:S(2)}, u32[]{:S(2)}) collective-permute-start(f32[16,512]{1,0:T(8,128)S(1)} %get-tuple-element.195), channel_id=1, source_target_pairs={{32,0},{64,32},{96,64},{128,96},{160,128},{192,160},{224,192},{256... | collective-permute-start | bytes 98312 | tf_op jit(solution)/shard_map/ppermute | solution.py:31
  25.6 1.0 copy-start.1
  25.6 28.8 %copy-start.5 = (s32[1,512]{1,0:T(1,128)S(1)}, s32[1,512]{1,0:T(1,128)}, u32[]{:S(2)}) copy-start(s32[1,512]{1,0:T(1,128)} %param.10) | copy-start | bytes 6148
  58.7 13.3 %collective-permute-start.2 = (f32[16,512]{1,0:T(8,128)S(1)}, f32[16,512]{1,0:T(8,128)S(1)}, u32[]{:S(2)}, u32[]{:S(2)}) collective-permute-start(f32[16,512]{1,0:T(8,128)S(1)} %get-tuple-element.192), channel_id=1, source_target_pairs={{32,0},{64,32},{96,64},{128,96},{160,128},{192,160},{224,192},{256... | collective-permute-start | bytes 98312 | tf_op jit(solution)/shard_map/ppermute | solution.py:31
  60.0 12.0 %collective-permute-start.3 = (f32[16,512]{1,0:T(8,128)S(1)}, f32[16,512]{1,0:T(8,128)S(1)}, u32[]{:S(2)}, u32[]{:S(2)}) collective-permute-start(f32[16,512]{1,0:T(8,128)S(1)} %get-tuple-element.193), channel_id=1, source_target_pairs={{0,32},{32,64},{64,96},{96,128},{128,160},{160,192},{192,224},{224... | collective-permute-start | bytes 98312 | tf_op jit(solution)/shard_map/ppermute | solution.py:30
  82.6 1.2 copy-start.2
  82.6 139.4 %reduce-scatter.2.cloned.1.call-start = ((), (), s32[]{:S(2)}) async-start(), calls=%async_computation.1 | async-start | bytes 2359296 | tf_op jit(solution)/shard_map/reduce_scatter | solution.py:90
  85.9 219.1 %all-reduce.7.cloned.1.call-start = ((), (), s32[]{:S(2)}) async-start(), calls=%async_computation.3 | async-start | bytes 4358144 | tf_op jit(solution)/shard_map/psum | solution.py:10
Sparse Core Ops, SparseCore 0:
  82.7 139.2 all-reduce.4
  224.6 80.4 all-reduce.6
Sparse Core Ops, SparseCore 1:
  86.0 42.6 reduce-scatter.1
